TPU v7x, 32 devices: a whole 2x2x4 slice. The times are simulated.
32 devices in a mesh: cable: 16 (over z, y, core), grid: 2 (over x).
Axes of the slice: x: 2, y: 2, z: 4, core: 2. Of those that a mesh axis runs over, the one named last changes fastest.
Arguments:
- green: bfloat16 [2, 4096, 4096], P(None, 'cable', 'grid'), may hold values from -6 to 6
- source_weight: float32 [4096], P('grid'), may hold values from 0.25 to 4
- observed: float32 [2, 2, 4096, 256], P(None, None, 'cable'), may hold values from -6 to 6
- amp_weight: float32 [2, 4096, 256], P(None, 'cable'), may hold values from 0.25 to 2
- pair_used: int32 [16, 2], P('cable'), may hold values 0 or 1
Outputs:
- adjoint: float32 [2, 4096, 4096], P(None, 'cable', 'grid')
- kernel: float32 [4096], P('grid')
All inputs are finite; a program needn't handle non-finite values. No bound on the sum of `pair_used` on one device may be relied on, other than what follows from the above.
Results may differ from a plain program's by a relative error of at most 0.0037.
Values may be sent and summed in bfloat16 or wider, within the bound.
A program may use at most 64 MiB of HBM per device.

v0:
```python
import math

import jax
import jax.numpy as jnp
from jax import lax
from jax.sharding import PartitionSpec as P


def shifted(block, axis, distance):
    devices = range(lax.axis_size(axis))
    route = [((i - distance) % len(devices), i) for i in devices]
    return lax.ppermute(block, axis, route)


def build_block(pair_resid):
    resid_real = pair_resid[0]
    resid_imag = pair_resid[1]
    upper_half = jnp.concatenate([resid_real, resid_imag], axis=1)
    lower_half = jnp.concatenate([-resid_imag, resid_real], axis=1)
    return jnp.concatenate([upper_half, lower_half], axis=0)


def residuals(corr, observed_rows, weight_rows, pair_used):
    mask_values = pair_used[0].astype(jnp.float32)
    scaled = mask_values[:, None, None, None] * weight_rows[:, None, :, :] * (corr - observed_rows)
    return scaled.astype(jnp.bfloat16)


def shards(green, source_weight, observed, amp_weight, pair_used):
    row_count = green.shape[1]
    col_count = green.shape[2]
    block_count = lax.axis_size("cable")
    grid_count = lax.axis_size("grid")
    inv_norm = 1.0 / math.sqrt(col_count * grid_count)
    kernel_scale = inv_norm / (2.0 * math.sqrt(2.0 * block_count))
    own_block = green.reshape(2 * row_count, col_count)
    near_blocks = []
    for offset in range(2):
        near_blocks.append(shifted(own_block, "cable", offset + 1))
    far_blocks = []
    for offset in range(2):
        far_blocks.append(shifted(own_block, "cable", -(offset + 1)))
    weighted = (own_block.astype(jnp.float32) * source_weight[None, :]).astype(jnp.bfloat16)
    partial_list = []
    for offset in range(2):
        products = lax.dot_general(
            weighted,
            near_blocks[offset],
            (((1,), (1,)), ((), ())),
            preferred_element_type=jnp.float32,
        )
        corr_real = products[:row_count, :row_count] + products[row_count:, row_count:]
        corr_imag = products[:row_count, row_count:] - products[row_count:, :row_count]
        partial_list.append(jnp.stack([corr_real, corr_imag]))
    partials = jnp.stack(partial_list)
    summed = lax.psum(partials, "grid")
    resid = residuals(inv_norm * summed, observed, amp_weight, pair_used)
    own_float = own_block.astype(jnp.float32)
    fields = jnp.zeros((2 * row_count, col_count), jnp.float32)
    kernel_part = jnp.zeros((col_count,), jnp.float32)
    for offset in range(2):
        resid_block = build_block(resid[offset])
        later_term = jnp.dot(resid_block, near_blocks[offset], preferred_element_type=jnp.float32)
        kernel_part = kernel_part + jnp.sum(own_float * later_term, axis=0)
        fields = fields + later_term
    for offset in range(2):
        arrived = shifted(resid[offset], "cable", -(offset + 1))
        resid_block = build_block(arrived)
        fields = fields + lax.dot_general(
            resid_block,
            far_blocks[offset],
            (((0,), (0,)), ((), ())),
            preferred_element_type=jnp.float32,
        )
    kernel = lax.psum(kernel_part, "cable") * kernel_scale
    adjoint = (inv_norm * source_weight[None, :] * fields).reshape(2, row_count, col_count)
    return (adjoint, kernel)


def solution(mesh):
    in_specs = (
        P(None, "cable", "grid"),
        P("grid"),
        P(None, None, "cable", None),
        P(None, "cable", None),
        P("cable", None),
    )
    out_specs = (P(None, "cable", "grid"), P("grid"))
    return jax.shard_map(shards, mesh=mesh, in_specs=in_specs, out_specs=out_specs, check_vma=False)
```

profile of v0, /device:TPU:0, one launch (start us, length us, event | category | flops | bytes accessed | tf_op | source)
XLA Modules:
  0.0 207.6 jit_solution(2422422331392514433)
XLA Ops:
  7.2 0.0 all-reduce.2.cloned.1.call-start
  7.2 0.0 copy-start.2
  7.2 0.0 copy-start.8
  7.2 0.5 collective-permute-start
  7.7 2.6 %collective-permute-start.1 = (bf16[512,2048]{1,0:T(8,128)(2,1)}, bf16[512,2048]{1,0:T(8,128)(2,1)S(1)}, u32[]{:S(2)}, u32[]{:S(2)}) collective-permute-start(bf16[512,2048]{1,0:T(8,128)(2,1)} %bitcast.54), channel_id=1, source_target_pairs={{28,0},{30,2},{0,4},{2,6},{4,8},{6,10},{8,12},{10,14},{12,16},{14,... | collective-permute-start | bytes 6291464 | tf_op jit(solution)/shard_map/ppermute | solution.py:12
  10.3 47.9 %collective-permute-done = bf16[512,2048]{1,0:T(8,128)(2,1)S(1)} collective-permute-done((bf16[512,2048]{1,0:T(8,128)(2,1)}, bf16[512,2048]{1,0:T(8,128)(2,1)S(1)}, u32[]{:S(2)}, u32[]{:S(2)}) %collective-permute-start) | collective-permute-done | bytes 2097184 | tf_op jit(solution)/shard_map/ppermute | solution.py:12
  58.2 0.0 copy-start.5
  58.2 3.6 %fusion.5 = f32[512,512]{1,0:T(8,128)S(1)} fusion(bf16[512,2048]{1,0:T(8,128)(2,1)S(1)} %collective-permute-done, bf16[512,2048]{1,0:T(8,128)(2,1)} %bitcast.55, f32[2048]{0:T(1024)} %param.6), kind=kOutput, calls=%fused_computation.8 | convolution fusion | flops 1076887552 | bytes 5251072 | tf_op jit(solution)/shard_map/dot_general | solution.py:46
  61.9 0.0 copy-done.5
  61.9 0.1 fusion.44
  61.9 0.0 collective-permute-done.1
  62.0 0.0 copy-done.2
  62.0 0.0 copy-done.8
  62.0 0.0 copy-start.3
  62.0 1.3 fusion.3
  63.3 0.0 copy-done.3
  63.3 0.1 fusion.42
  63.4 0.1 maximum_bitcast_fusion
  63.5 0.0 copy-start.9
  63.5 0.0 copy-start.7
  63.5 1.1 pad_maximum_fusion
  64.6 0.0 all-reduce.2.cloned.1.call-update
  64.6 21.4 %collective-permute-start.3 = (bf16[512,2048]{1,0:T(8,128)(2,1)S(1)}, bf16[512,2048]{1,0:T(8,128)(2,1)}, u32[]{:S(2)}, u32[]{:S(2)}) collective-permute-start(bf16[512,2048]{1,0:T(8,128)(2,1)S(1)} %bitcast.57), channel_id=1, source_target_pairs={{2,0},{4,2},{6,4},{8,6},{10,8},{12,10},{14,12},{16,14},{18,16},{20... | collective-permute-start | bytes 6291464 | tf_op jit(solution)/shard_map/ppermute | solution.py:12
  86.0 1.4 collective-permute-start.5
  87.4 0.0 copy-done.9
  87.4 0.0 copy-done.7
  87.4 0.1 broadcast_multiply_fusion
  87.5 35.4 %all-reduce.2.cloned.1.call-done = f32[2,2,256,256]{3,2,1,0:T(8,128)} async-done(((f32[2,2,256,256]{3,2,1,0:T(8,128)}), f32[2,2,256,256]{3,2,1,0:T(8,128)}) %all-reduce.2.cloned.1.call-update) | async-done | bytes 1048592 | tf_op jit(solution)/shard_map/psum | solution.py:56
  122.9 1.7 multiply_convert_fusion
  124.6 0.0 copy-start.6
  124.7 3.7 %collective-permute-start.2 = (bf16[2,256,256]{2,1,0:T(8,128)(2,1)S(1)}, bf16[2,256,256]{2,1,0:T(8,128)(2,1)S(1)}, u32[]{:S(2)}, u32[]{:S(2)}) collective-permute-start(bf16[2,256,256]{2,1,0:T(8,128)(2,1)S(1)} %get-tuple-element.9), channel_id=1, source_target_pairs={{2,0},{4,2},{6,4},{8,6},{10,8},{12,10},{14,12},{16,14},{18,16},{20... | collective-permute-start | bytes 786440 | tf_op jit(solution)/shard_map/ppermute | solution.py:12
  128.5 0.6 collective-permute-start.4
  129.1 0.0 copy-done.6
  129.1 1.3 fusion.7
  130.4 0.0 copy-start
  130.4 0.3 copy-done.4
  130.7 3.6 %fusion.2 = (f32[2048]{0:T(1024)S(1)}, f32[2048]{0:T(1024)S(1)}, f32[512,2048]{1,0:T(8,128)}) fusion(bf16[2,256,2048]{2,1,0:T(8,128)(2,1)S(1)} %copy-done.2, f32[512,2048]{1,0:T(8,128)S(1)} %fusion.7, bf16[512,2048]{1,0:T(8,128)(2,1)S(1)} %copy-done.4, bf16[256,256]{1,0:T(8,128)(2,1)S(1)} %get-tuple-element.11, bf16[256,256]{1,0:T(8,128)(2,1)S(1)} %get-tuple-element.14, ...), kind=kOutput, calls=%fused_computation.5 | convolution fusion | flops 1081077760 | bytes 12992512 | tf_op jit(solution)/shard_map/dot_general | solution.py:63
  134.3 0.0 copy-done
  134.3 55.9 %psum.15 = f32[2048]{0:T(1024)S(1)} all-reduce(f32[2048]{0:T(1024)S(1)} %add.27), channel_id=1, replica_groups=mesh['cable'=16,'grid'=2] {'cable'}, use_global_device_ids=true, to_apply=%region_3.0 | all-reduce | flops 2048 | bytes 16384 | tf_op jit(solution)/shard_map/psum | solution.py:75
  190.2 0.6 broadcast_multiply_fusion.1
  190.8 0.0 collective-permute-done.2
  190.8 0.0 collective-permute-done.4
  190.9 0.0 collective-permute-done.3
  190.9 0.0 copy-start.1
  190.9 3.0 %fusion.23 = f32[512,2048]{1,0:T(8,128)S(1)} fusion(bf16[512,2048]{1,0:T(8,128)(2,1)} %collective-permute-done.3, bf16[256,256]{1,0:T(8,128)(2,1)S(1)} %get-tuple-element.19, bf16[256,256]{1,0:T(8,128)(2,1)S(1)} %fusion.51, bf16[256,256]{1,0:T(8,128)(2,1)S(1)} %get-tuple-element.18), kind=kOutput, calls=%fused_computation.29 | convolution fusion | flops 1075838976 | bytes 6684672 | tf_op jit(solution)/shard_map/dot_general | solution.py:69
  194.0 0.0 collective-permute-done.5
  194.0 0.0 copy-done.1
  194.0 6.8 %add_multiply_fusion = f32[512,2048]{1,0:T(8,128)} fusion(f32[512,2048]{1,0:T(8,128)S(1)} %fusion.23, f32[512,2048]{1,0:T(8,128)S(1)} %copy-done.1, f32[512,2048]{1,0:T(8,128)} %get-tuple-element.20, f32[2048]{0:T(1024)S(1)} %broadcast_multiply_fusion.2, bf16[512,2048]{1,0:T(8,128)(2,1)} %collective-permute-done.5, ...), kind=kOutput, calls=%fused_computation.6 | convolution fusion | flops 1080033280 | bytes 19275776 | tf_op jit(solution)/shard_map/dot_general | solution.py:69
  (11 shorter events, 0.2 us)
Async XLA Ops:
  7.2 115.7 %all-reduce.2.cloned.1.call-start = ((), (), s32[]{:S(2)}) async-start(), calls=%async_computation | async-start | bytes 2097152 | tf_op jit(solution)/shard_map/psum | solution.py:56
  7.2 54.7 %copy-start.2 = (bf16[2,256,2048]{2,1,0:T(8,128)(2,1)S(1)}, bf16[2,256,2048]{2,1,0:T(8,128)(2,1)}, u32[]{:S(2)}) copy-start(bf16[2,256,2048]{2,1,0:T(8,128)(2,1)} %param.5) | copy-start | bytes 6291460
  7.2 54.7 %copy-start.8 = (f32[2048]{0:T(1024)S(1)}, f32[2048]{0:T(1024)}, u32[]{:S(2)}) copy-start(f32[2048]{0:T(1024)} %param.6) | copy-start | bytes 24580
  7.2 51.0 %collective-permute-start = (bf16[512,2048]{1,0:T(8,128)(2,1)}, bf16[512,2048]{1,0:T(8,128)(2,1)S(1)}, u32[]{:S(2)}, u32[]{:S(2)}) collective-permute-start(bf16[512,2048]{1,0:T(8,128)(2,1)} %bitcast.53), channel_id=1, source_target_pairs={{30,0},{0,2},{2,4},{4,6},{6,8},{8,10},{10,12},{12,14},{14,16},{16,... | collective-permute-start | bytes 6291464 | tf_op jit(solution)/shard_map/ppermute | solution.py:12
  7.7 54.2 %collective-permute-start.1 = (bf16[512,2048]{1,0:T(8,128)(2,1)}, bf16[512,2048]{1,0:T(8,128)(2,1)S(1)}, u32[]{:S(2)}, u32[]{:S(2)}) collective-permute-start(bf16[512,2048]{1,0:T(8,128)(2,1)} %bitcast.54), channel_id=1, source_target_pairs={{28,0},{30,2},{0,4},{2,6},{4,8},{6,10},{8,12},{10,14},{12,16},{14,... | collective-permute-start | bytes 6291464 | tf_op jit(solution)/shard_map/ppermute | solution.py:12
  58.2 3.6 %copy-start.5 = (bf16[512,2048]{1,0:T(8,128)(2,1)}, bf16[512,2048]{1,0:T(8,128)(2,1)S(1)}, u32[]{:S(2)}) copy-start(bf16[512,2048]{1,0:T(8,128)(2,1)S(1)} %collective-permute-done) | copy-start | bytes 6291460
  62.0 1.3 copy-start.3
  63.5 23.9 %copy-start.9 = (s32[1,2]{1,0:T(1,128)S(1)}, s32[1,2]{1,0:T(1,128)}, u32[]{:S(2)}) copy-start(s32[1,2]{1,0:T(1,128)} %param.9) | copy-start | bytes 28
  63.5 23.9 %copy-start.7 = (f32[2,256,256]{2,1,0:T(8,128)S(1)}, f32[2,256,256]{2,1,0:T(8,128)}, u32[]{:S(2)}) copy-start(f32[2,256,256]{2,1,0:T(8,128)} %param.8) | copy-start | bytes 1572868
  64.6 126.3 %collective-permute-start.3 = (bf16[512,2048]{1,0:T(8,128)(2,1)S(1)}, bf16[512,2048]{1,0:T(8,128)(2,1)}, u32[]{:S(2)}, u32[]{:S(2)}) collective-permute-start(bf16[512,2048]{1,0:T(8,128)(2,1)S(1)} %bitcast.57), channel_id=1, source_target_pairs={{2,0},{4,2},{6,4},{8,6},{10,8},{12,10},{14,12},{16,14},{18,16},{20... | collective-permute-start | bytes 6291464 | tf_op jit(solution)/shard_map/ppermute | solution.py:12
  86.0 108.0 %collective-permute-start.5 = (bf16[512,2048]{1,0:T(8,128)(2,1)S(1)}, bf16[512,2048]{1,0:T(8,128)(2,1)}, u32[]{:S(2)}, u32[]{:S(2)}) collective-permute-start(bf16[512,2048]{1,0:T(8,128)(2,1)S(1)} %bitcast.58), channel_id=1, source_target_pairs={{4,0},{6,2},{8,4},{10,6},{12,8},{14,10},{16,12},{18,14},{20,16},{2... | collective-permute-start | bytes 6291464 | tf_op jit(solution)/shard_map/ppermute | solution.py:12
  124.6 4.5 %copy-start.6 = (bf16[512,2048]{1,0:T(8,128)(2,1)S(1)}, bf16[512,2048]{1,0:T(8,128)(2,1)}, u32[]{:S(2)}) copy-start(bf16[512,2048]{1,0:T(8,128)(2,1)} %copy-done.5) | copy-start | bytes 6291460
  124.7 66.1 %collective-permute-start.2 = (bf16[2,256,256]{2,1,0:T(8,128)(2,1)S(1)}, bf16[2,256,256]{2,1,0:T(8,128)(2,1)S(1)}, u32[]{:S(2)}, u32[]{:S(2)}) collective-permute-start(bf16[2,256,256]{2,1,0:T(8,128)(2,1)S(1)} %get-tuple-element.9), channel_id=1, source_target_pairs={{2,0},{4,2},{6,4},{8,6},{10,8},{12,10},{14,12},{16,14},{18,16},{20... | collective-permute-start | bytes 786440 | tf_op jit(solution)/shard_map/ppermute | solution.py:12
  128.5 62.4 %collective-permute-start.4 = (bf16[2,256,256]{2,1,0:T(8,128)(2,1)S(1)}, bf16[2,256,256]{2,1,0:T(8,128)(2,1)S(1)}, u32[]{:S(2)}, u32[]{:S(2)}) collective-permute-start(bf16[2,256,256]{2,1,0:T(8,128)(2,1)S(1)} %get-tuple-element.8), channel_id=1, source_target_pairs={{4,0},{6,2},{8,4},{10,6},{12,8},{14,10},{16,12},{18,14},{20,16},{2... | collective-permute-start | bytes 786440 | tf_op jit(solution)/shard_map/ppermute | solution.py:12
  129.1 1.6 copy-start.4
  130.4 3.9 %copy-start = (f32[512,2048]{1,0:T(8,128)}, f32[512,2048]{1,0:T(8,128)S(1)}, u32[]{:S(2)}) copy-start(f32[512,2048]{1,0:T(8,128)S(1)} %fusion.7) | copy-start | bytes 12582916
  190.9 3.1 %copy-start.1 = (f32[512,2048]{1,0:T(8,128)S(1)}, f32[512,2048]{1,0:T(8,128)}, u32[]{:S(2)}) copy-start(f32[512,2048]{1,0:T(8,128)} %copy-done) | copy-start | bytes 12582916
Sparse Core Ops, SparseCore 0:
  64.7 58.1 all-reduce.1
where the time goes:
time: 208 us
  waiting for transfers between devices  83.3 us (40%)
  blocking collectives  55.9 us (27%)
  starting transfers between devices  30.3 us (15%)
  matrix products  19.6 us (9%)
  between operations  14.3 us (7%)
  other arithmetic  3.77 us (2%)
    psum x1, blocking collectives, shards(): kernel = lax.psum(kernel_part, 'cable') * kernel_scale  55.9 us
    ppermute x6, waiting for transfers between devices, shifted(): return lax.ppermute(block, axis, route)  47.9 us
    psum x1, waiting for transfers between devices, shards(): summed = lax.psum(partials, 'grid')  35.4 us
    ppermute x6, starting transfers between devices, shifted(): return lax.ppermute(block, axis, route)  30.3 us
    dot_general x2, matrix products, shards(): lax.dot_general(resid_block, far_blocks[offset], (((0,), (0,)), ((), ()))...  9.81 us
    dot_general x2, matrix products, shards(): lax.dot_general(weighted, near_blocks[offset], (((1,), (1,)), ((), ())),...  4.93 us
    dot_general x2, matrix products, shards(): jnp.dot(resid_block, near_blocks[offset], preferred_element_type=jnp.floa...  4.85 us
  transfers between devices with their start and end apart: 7, of which 2 were waited for; matrix products, arithmetic and copies ran while one was open for 7% of the time, Pallas kernels for 0%

commit v1 on v0

v1 whole, which is shorter than its diff:
```python
import functools
import math

import jax
import jax.numpy as jnp
from jax import lax
from jax.experimental import pallas as pl
from jax.experimental.pallas import tpu as pltpu
from jax.sharding import PartitionSpec as P

MESH = pl.DeviceIdType.MESH
E1, E2, L1, L2 = 0, 1, 2, 3
CHUNKS = 8
HALVES = 2
LAG = 2


def body(cfg, green, weight, observed, amp, used, fields_out, kernel_out,
         near, weighted, corr_own, corr_in, resid_own, resid_in, later_mat, early_mat, acc, parts,
         mate_send, mate_recv, sib_send, sib_recv, far_send, far_recv, pass_send, pass_recv,
         corr_send, corr_recv, resid_send, resid_recv, part_send, part_recv, out_sem):
    n, ng, inv_norm, kernel_scale = cfg
    rows, cols = green.shape[1], green.shape[2]
    half_rows = rows // HALVES
    chunk_rows = rows // CHUNKS
    tile = min(512, cols)
    me = lax.axis_index("cable")
    gx = lax.axis_index("grid")
    core = lax.rem(me, 2)
    chip_odd = lax.rem(me // 2, 2)
    sign = 1 - 2 * chip_odd
    sibling = me + 1 - 2 * core
    mate = lax.rem(me + 2 * sign + n, n)
    onward = lax.rem(me + 4 * sign + n, n)
    mate_slot = L2 - 2 * chip_odd
    far_slot = E2 + 2 * chip_odd
    pass_from = L2 - 2 * core
    pass_to = L1 - 2 * core
    sib_to = E1 + 2 * core
    pass_is_mate = core == chip_odd

    barrier = pltpu.get_barrier_semaphore()

    def greet_cable(step, carry):
        pl.semaphore_signal(barrier, inc=1, device_id=(lax.rem(me + step, n), gx), device_id_type=MESH)
        return carry

    lax.fori_loop(1, n, greet_cable, 0)
    for step in range(1, ng):
        pl.semaphore_signal(barrier, inc=1, device_id=(me, lax.rem(gx + step, ng)), device_id_type=MESH)
    pl.semaphore_wait(barrier, n - 1 + ng - 1)

    def chunk(t):
        return pl.ds(t * chunk_rows, chunk_rows)

    def remote(src, dst, send, recv, cable, grid):
        return pltpu.make_async_remote_copy(
            src_ref=src, dst_ref=dst, send_sem=send, recv_sem=recv,
            device_id=(cable, grid), device_id_type=MESH)

    def to_mate(t):
        return remote(green.at[:, chunk(t), :], near.at[far_slot, :, chunk(t), :],
                      mate_send.at[t], mate_recv.at[t], mate, gx)

    def to_sib(h):
        spot = pl.ds(h * half_rows, half_rows)
        return remote(green.at[:, spot, :], near.at[sib_to, :, spot, :],
                      sib_send.at[h], sib_recv.at[h], sibling, gx)

    def to_far(t):
        return remote(near.at[mate_slot, :, chunk(t), :], near.at[far_slot, :, chunk(t), :],
                      far_send.at[t], far_recv.at[t], onward, gx)

    def to_pass(t):
        return remote(near.at[pass_from, :, chunk(t), :], near.at[pass_to, :, chunk(t), :],
                      pass_send.at[t], pass_recv.at[t], sibling, gx)

    def got_mate(t):
        remote(green.at[:, chunk(t), :], near.at[mate_slot, :, chunk(t), :],
               mate_send.at[t], mate_recv.at[t], mate, gx).wait_recv()

    def got_sib(h):
        spot = pl.ds(h * half_rows, half_rows)
        remote(green.at[:, spot, :], near.at[2 - sib_to, :, spot, :],
               sib_send.at[h], sib_recv.at[h], sibling, gx).wait_recv()

    def got_pass(t):
        remote(near.at[pass_from, :, chunk(t), :], near.at[2 - pass_to, :, chunk(t), :],
               pass_send.at[t], pass_recv.at[t], sibling, gx).wait_recv()

    def corr_copy(h, step):
        return remote(corr_own.at[h], corr_in.at[h, step - 1],
                      corr_send.at[h, step - 1], corr_recv.at[h, step - 1],
                      me, lax.rem(gx + step, ng))

    def resid_copy(h, o):
        return remote(resid_own.at[h, o], resid_in.at[h, o],
                      resid_send.at[h, o], resid_recv.at[h, o],
                      lax.rem(me - (o + 1) + n, n), gx)

    def correlate(h):
        spot = pl.ds(h * half_rows, half_rows)
        for o in range(2):
            other = near[o, :, spot, :].reshape(2 * half_rows, cols)
            prod = lax.dot_general(weighted[...], other, (((1,), (1,)), ((), ())),
                                   preferred_element_type=jnp.float32)
            corr_own[h, o, 0] = prod[:rows, :half_rows] + prod[rows:, half_rows:]
            corr_own[h, o, 1] = prod[:rows, half_rows:] - prod[rows:, :half_rows]
        for step in range(1, ng):
            corr_copy(h, step).start()

    def residual(h):
        for step in range(1, ng):
            corr_copy(h, step).wait()
        for o in range(2):
            mask = used[0, o].astype(jnp.float32) * amp[o, :, h * half_rows:(h + 1) * half_rows]
            pair = []
            for part in range(2):
                total = corr_own[h, o, part]
                for step in range(1, ng):
                    total = total + corr_in[h, step - 1, o, part]
                pair.append(mask * (inv_norm * total - observed[o, part, :, h * half_rows:(h + 1) * half_rows]))
            real, imag = pair
            resid_own[h, o, 0] = real.T.astype(jnp.bfloat16)
            resid_own[h, o, 1] = imag.T.astype(jnp.bfloat16)
            resid_copy(h, o).start()
            left = o * 2 * half_rows
            real16 = real.astype(jnp.bfloat16)
            imag16 = imag.astype(jnp.bfloat16)
            minus16 = (-imag).astype(jnp.bfloat16)
            later_mat[h, 0:rows, left:left + half_rows] = real16
            later_mat[h, 0:rows, left + half_rows:left + 2 * half_rows] = imag16
            later_mat[h, rows:2 * rows, left:left + half_rows] = minus16
            later_mat[h, rows:2 * rows, left + half_rows:left + 2 * half_rows] = real16

    def gather_early(h):
        for o in range(2):
            resid_copy(h, o).wait_recv()
            left = o * 2 * rows
            real = resid_in[h, o, 0]
            imag = resid_in[h, o, 1]
            early_mat[h, 0:half_rows, left:left + rows] = real
            early_mat[h, 0:half_rows, left + rows:left + 2 * rows] = -imag
            early_mat[h, half_rows:2 * half_rows, left:left + rows] = imag
            early_mat[h, half_rows:2 * half_rows, left + rows:left + 2 * rows] = real

    def later_terms(h):
        spot = pl.ds(h * half_rows, half_rows)

        def step(i, carry):
            at = pl.ds(pl.multiple_of(i * tile, tile), tile)
            other = near[E1:E2 + 1, :, spot, at].reshape(4 * half_rows, tile)
            term = jnp.dot(later_mat[h], other, preferred_element_type=jnp.float32).reshape(2, rows, tile)
            share = jnp.sum(green[:, :, at].astype(jnp.float32) * term, axis=(0, 1)).reshape(1, tile)
            if h == 0:
                acc[:, :, at] = term
                parts[me, :, at] = share
            else:
                acc[:, :, at] += term
                parts[me, :, at] += share
            return carry

        lax.fori_loop(0, cols // tile, step, 0)

    def early_terms(h):
        spot = pl.ds(h * half_rows, half_rows)

        def step(i, carry):
            at = pl.ds(pl.multiple_of(i * tile, tile), tile)
            other = near[L1:L2 + 1, :, :, at].reshape(4 * rows, tile)
            term = jnp.dot(early_mat[h], other, preferred_element_type=jnp.float32).reshape(2, half_rows, tile)
            acc[:, spot, at] += term
            return carry

        lax.fori_loop(0, cols // tile, step, 0)

    def scale_rows(h):
        spot = pl.ds(h * half_rows, half_rows)
        acc[:, spot, :] = acc[:, spot, :] * (inv_norm * weight[...]).reshape(1, 1, cols)

    def out_copy(h):
        spot = pl.ds(h * half_rows, half_rows)
        return pltpu.make_async_copy(acc.at[:, spot, :], fields_out.at[:, spot, :], out_sem.at[h])

    for t in range(CHUNKS):
        to_mate(t).start()
    for h in range(HALVES):
        to_sib(h).start()
    weighted[...] = (green[...].astype(jnp.float32) * weight[...].reshape(1, 1, cols)).astype(
        jnp.bfloat16).reshape(2 * rows, cols)
    for h in range(HALVES):
        got_sib(h)

    per_half = CHUNKS // HALVES

    def far_step(t):
        to_far(t).wait_recv()

        @pl.when(jnp.logical_not(pass_is_mate))
        def _():
            to_pass(t).start()

    for t in range(CHUNKS):
        got_mate(t)
        to_far(t).start()

        @pl.when(pass_is_mate)
        def _():
            to_pass(t).start()

        if t >= LAG:
            far_step(t - LAG)
        if t - LAG == per_half - 1:
            for u in range(per_half):
                got_pass(u)
            correlate(0)
    residual(0)
    for t in range(CHUNKS - LAG, CHUNKS):
        far_step(t)
    for u in range(per_half, CHUNKS):
        got_pass(u)
    correlate(1)
    later_terms(0)
    gather_early(0)
    early_terms(0)
    residual(1)
    later_terms(1)

    def part_copy(step):
        target = lax.rem(me + step, n)
        return remote(parts.at[me], parts.at[me], part_send.at[step], part_recv.at[me], target, gx)

    def part_start(step, carry):
        part_copy(step).start()
        return carry

    lax.fori_loop(1, n, part_start, 0)
    scale_rows(0)
    out_copy(0).start()
    gather_early(1)
    early_terms(1)
    scale_rows(1)
    out_copy(1).start()

    def part_wait(step, carry):
        source = lax.rem(me + step, n)
        remote(parts.at[me], parts.at[source], part_send.at[step], part_recv.at[source], source, gx).wait()
        return carry

    lax.fori_loop(1, n, part_wait, 0)

    def add_part(i, total):
        return total + parts[i]

    kernel_out[...] = kernel_scale * lax.fori_loop(1, n, add_part, parts[0])

    for t in range(CHUNKS):
        to_mate(t).wait_send()
        to_far(t).wait_send()
        to_pass(t).wait_send()
    for h in range(HALVES):
        to_sib(h).wait_send()
        for o in range(2):
            resid_copy(h, o).wait_send()
        out_copy(h).wait()


def shards(green, source_weight, observed, amp_weight, pair_used):
    rows, cols = green.shape[1], green.shape[2]
    n = lax.axis_size("cable")
    ng = lax.axis_size("grid")
    inv_norm = 1.0 / math.sqrt(cols * ng)
    kernel_scale = inv_norm / (2.0 * math.sqrt(2.0 * n))
    half = rows // HALVES
    peers = max(ng - 1, 1)
    f32, bf16 = jnp.float32, jnp.bfloat16
    dma = pltpu.SemaphoreType.DMA
    vmem = pl.BlockSpec(memory_space=pltpu.VMEM)
    adjoint, kernel = pl.pallas_call(
        functools.partial(body, (n, ng, inv_norm, kernel_scale)),
        out_shape=(jax.ShapeDtypeStruct((2, rows, cols), f32), jax.ShapeDtypeStruct((1, cols), f32)),
        in_specs=[vmem, vmem, vmem, vmem, pl.BlockSpec(memory_space=pltpu.SMEM)],
        out_specs=(pl.BlockSpec(memory_space=pl.ANY), vmem),
        scratch_shapes=[
            pltpu.VMEM((4, 2, rows, cols), bf16),
            pltpu.VMEM((2 * rows, cols), bf16),
            pltpu.VMEM((HALVES, 2, 2, rows, half), f32),
            pltpu.VMEM((HALVES, peers, 2, 2, rows, half), f32),
            pltpu.VMEM((HALVES, 2, 2, half, rows), bf16),
            pltpu.VMEM((HALVES, 2, 2, half, rows), bf16),
            pltpu.VMEM((HALVES, 2 * rows, 4 * half), bf16),
            pltpu.VMEM((HALVES, 2 * half, 4 * rows), bf16),
            pltpu.VMEM((2, rows, cols), f32),
            pltpu.VMEM((n, 1, cols), f32),
            dma((CHUNKS,)), dma((CHUNKS,)),
            dma((HALVES,)), dma((HALVES,)),
            dma((CHUNKS,)), dma((CHUNKS,)),
            dma((CHUNKS,)), dma((CHUNKS,)),
            dma((HALVES, peers)), dma((HALVES, peers)),
            dma((HALVES, 2)), dma((HALVES, 2)),
            dma((n,)), dma((n,)),
            dma((HALVES,)),
        ],
        compiler_params=pltpu.CompilerParams(
            collective_id=0, has_side_effects=True, vmem_limit_bytes=56 * 1024 * 1024),
        cost_estimate=pl.CostEstimate(flops=24 * rows * rows * cols * 2, bytes_accessed=20 * rows * cols, transcendentals=0),
    )(green, source_weight.reshape(1, cols), observed, amp_weight, pair_used)
    return (adjoint, kernel.reshape(cols))


def solution(mesh):
    in_specs = (
        P(None, "cable", "grid"),
        P("grid"),
        P(None, None, "cable", None),
        P(None, "cable", None),
        P("cable", None),
    )
    out_specs = (P(None, "cable", "grid"), P("grid"))
    return jax.shard_map(shards, mesh=mesh, in_specs=in_specs, out_specs=out_specs, check_vma=False)
```

time: 208 us -> 95.4 us (0.46)
  Pallas kernels: 0 us -> 89.3 us
  waiting for transfers between devices: 83.3 us -> 0 us
  blocking collectives: 55.9 us -> 0 us
  starting transfers between devices: 30.3 us -> 0 us
  matrix products: 19.6 us -> 0 us
  between operations: 14.3 us -> 0.65 us
  local copies, waits for them, and re-layouts: 0.5 us -> 5.31 us
  other arithmetic: 3.77 us -> 0 us
    pallas_call x0 -> x1, Pallas kernels: none -> 89.3 us  [shards(): pl.pallas_call(functools.partial(body, (n, ng, inv_norm, kernel_scale)),...]
    psum x1 -> x0, blocking collectives: 55.9 us -> none  [shards(): kernel = lax.psum(kernel_part, 'cable') * kernel_scale]
    ppermute x6 -> x0, waiting for transfers between devices: 47.9 us -> none  [shifted(): return lax.ppermute(block, axis, route)]
    psum x1 -> x0, waiting for transfers between devices: 35.4 us -> none  [shards(): summed = lax.psum(partials, 'grid')]
    ppermute x6 -> x0, starting transfers between devices: 30.3 us -> none  [shifted(): return lax.ppermute(block, axis, route)]
    dot_general x6 -> x0, matrix products: 19.6 us -> none  [the longest x2 9.81 us: shards(): lax.dot_general(resid_block, far_blocks[offset], (((0,), (0,)), ((), ()))...]
    unnamed x20 -> x4, local copies, waits for them, and re-layouts: 0.38 us -> 5.31 us
  transfers between devices with their start and end apart: 7 -> 0, of which waited for: 2 -> 0; matrix products, arithmetic and copies ran while one was open for 7% -> 0% of each run, Pallas kernels for 0% -> 0%
where the time goes in v1:
time: 95.4 us; the launch traced here: 95.3 us
  Pallas kernels  89.3 us (94%)
  local copies, waits for them, and re-layouts  5.31 us (6%)
    pallas_call x1, Pallas kernels, shards(): pl.pallas_call(functools.partial(body, (n, ng, inv_norm, kernel_scale)),...  89.3 us
    unnamed x4, local copies, waits for them, and re-layouts  5.31 us

profile of v1, /device:TPU:0, one launch (start us, length us, event | category | flops | bytes accessed | tf_op | source)
XLA Modules:
  0.0 95.3 jit_solution(15671517838232606912)
XLA Ops:
  0.6 89.3 %shard_map.68 = (f32[2,256,2048]{2,1,0:T(8,128)}, f32[1,2048]{1,0:T(1,128)}) custom-call(bf16[2,256,2048]{2,1,0:T(8,128)(2,1)} %green.1, f32[1,2048]{1,0:T(1,128)} %bitcast.3, f32[2,2,256,256]{3,2,1,0:T(8,128)} %observed.1, f32[2,256,256]{2,1,0:T(8,128)} %amp.1, s32[1,2]{1,0:T(1,128)} %used.1), custom_call_target="tpu_custom_call" | custom-call | flops 6442450944 | bytes 10485760 | tf_op jit(solution)/shard_map/pallas_call | solution.py:279
  90.0 0.0 copy-start
  90.0 4.7 %copy.9 = f32[2,256,2048]{2,1,0:T(8,128)} copy(f32[2,256,2048]{2,1,0:T(8,128)} %get-tuple-element.8) | data formatting | bytes 8388608
  94.7 0.0 copy-done
  94.7 0.6 copy.10
Async XLA Ops:
  90.0 4.7 %copy-start = (f32[1,2048]{1,0:T(1,128)S(1)}, f32[1,2048]{1,0:T(1,128)}, u32[]{:S(2)}) copy-start(f32[1,2048]{1,0:T(1,128)} %get-tuple-element.5) | copy-start | bytes 24580

commit v2 on v1

v2 whole, which is shorter than its diff:
```python
import functools
import math

import jax
import jax.numpy as jnp
from jax import lax
from jax.experimental import pallas as pl
from jax.experimental.pallas import tpu as pltpu
from jax.sharding import PartitionSpec as P

MESH = pl.DeviceIdType.MESH
E1, E2, L1, L2 = 0, 1, 2, 3
CHUNKS = 16
UNITS = 4
HALVES = 2
LAG = 3


def body(cfg, green, weight, observed, amp, used, acc, kernel_out,
         own, obs_in, amp_in, obs_t, amp_t, near, weighted, corr_own, corr_in, resid_own, resid_in, later_mat, early_mat, parts,
         mate_send, mate_recv, sib_send, sib_recv, far_send, far_recv, pass_send, pass_recv,
         corr_send, corr_recv, resid_send, resid_recv, part_send, part_recv, load_sem):
    n, ng, inv_norm, kernel_scale = cfg
    rows, cols = green.shape[1], green.shape[2]
    half_rows = rows // HALVES
    unit = rows // UNITS
    chunk_rows = rows // CHUNKS
    tile = min(512, cols)
    me = lax.axis_index("cable")
    gx = lax.axis_index("grid")
    core = lax.rem(me, 2)
    chip_odd = lax.rem(me // 2, 2)
    sign = 1 - 2 * chip_odd
    sibling = me + 1 - 2 * core
    mate = lax.rem(me + 2 * sign + n, n)
    onward = lax.rem(me + 4 * sign + n, n)
    mate_slot = L2 - 2 * chip_odd
    far_slot = E2 + 2 * chip_odd
    pass_from = L2 - 2 * core
    pass_to = L1 - 2 * core
    sib_to = E1 + 2 * core
    pass_is_mate = core == chip_odd

    barrier = pltpu.get_barrier_semaphore()

    def greet_cable(step, carry):
        pl.semaphore_signal(barrier, inc=1, device_id=(lax.rem(me + step, n), gx), device_id_type=MESH)
        return carry

    lax.fori_loop(1, n, greet_cable, 0)
    for step in range(1, ng):
        pl.semaphore_signal(barrier, inc=1, device_id=(me, lax.rem(gx + step, ng)), device_id_type=MESH)
    loads = [pltpu.make_async_copy(src, dst, load_sem.at[i])
             for i, (src, dst) in enumerate(((green, own), (observed, obs_in), (amp, amp_in)))]
    for copy in loads:
        copy.start()
    pl.semaphore_wait(barrier, n - 1 + ng - 1)

    def rows_of(u):
        return slice(u * unit, (u + 1) * unit)

    def chunk(t):
        return pl.ds(t * chunk_rows, chunk_rows)

    def remote(src, dst, send, recv, cable, grid):
        return pltpu.make_async_remote_copy(
            src_ref=src, dst_ref=dst, send_sem=send, recv_sem=recv,
            device_id=(cable, grid), device_id_type=MESH)

    def to_mate(t):
        return remote(green.at[:, chunk(t), :], near.at[far_slot, :, chunk(t), :],
                      mate_send.at[t], mate_recv.at[t], mate, gx)

    def to_sib(h):
        spot = pl.ds(h * half_rows, half_rows)
        return remote(green.at[:, spot, :], near.at[sib_to, :, spot, :],
                      sib_send.at[h], sib_recv.at[h], sibling, gx)

    def to_far(t):
        return remote(near.at[mate_slot, :, chunk(t), :], near.at[far_slot, :, chunk(t), :],
                      far_send.at[t], far_recv.at[t], onward, gx)

    def to_pass(t):
        return remote(near.at[pass_from, :, chunk(t), :], near.at[pass_to, :, chunk(t), :],
                      pass_send.at[t], pass_recv.at[t], sibling, gx)

    def got_mate(t):
        remote(green.at[:, chunk(t), :], near.at[mate_slot, :, chunk(t), :],
               mate_send.at[t], mate_recv.at[t], mate, gx).wait_recv()

    def got_sib(h):
        spot = pl.ds(h * half_rows, half_rows)
        remote(green.at[:, spot, :], near.at[2 - sib_to, :, spot, :],
               sib_send.at[h], sib_recv.at[h], sibling, gx).wait_recv()

    def got_pass(t):
        remote(near.at[pass_from, :, chunk(t), :], near.at[2 - pass_to, :, chunk(t), :],
               pass_send.at[t], pass_recv.at[t], sibling, gx).wait_recv()

    def corr_copy(u, step):
        return remote(corr_own.at[u], corr_in.at[u, step - 1],
                      corr_send.at[u, step - 1], corr_recv.at[u, step - 1],
                      me, lax.rem(gx + step, ng))

    def resid_copy(u, o):
        return remote(resid_own.at[u, o], resid_in.at[u, o],
                      resid_send.at[u, o], resid_recv.at[u, o],
                      lax.rem(me - (o + 1) + n, n), gx)

    def correlate(u):
        other = near[E1:E2 + 1, :, rows_of(u), :].reshape(4 * unit, cols)
        prod = lax.dot_general(other, weighted[...], (((1,), (1,)), ((), ())),
                               preferred_element_type=jnp.float32)
        for o in range(2):
            from_real = prod[2 * o * unit:(2 * o + 1) * unit]
            from_imag = prod[(2 * o + 1) * unit:(2 * o + 2) * unit]
            corr_own[u, o, 0] = from_real[:, :rows] + from_imag[:, rows:]
            corr_own[u, o, 1] = from_imag[:, :rows] - from_real[:, rows:]
        for step in range(1, ng):
            corr_copy(u, step).start()

    def fill(mat, top, left, real, imag):
        mat[top:top + unit, left:left + rows] = real
        mat[top:top + unit, left + rows:left + 2 * rows] = -imag
        mat[top + unit:top + 2 * unit, left:left + rows] = imag
        mat[top + unit:top + 2 * unit, left + rows:left + 2 * rows] = real

    def residual(u):
        for step in range(1, ng):
            corr_copy(u, step).wait()
        for o in range(2):
            pair = []
            for part in range(2):
                total = corr_own[u, o, part]
                for step in range(1, ng):
                    total = total + corr_in[u, step - 1, o, part]
                value = amp_t[o, rows_of(u), :] * (inv_norm * total - obs_t[o, part, rows_of(u), :])
                pair.append(value.astype(jnp.bfloat16))
            resid_own[u, o, 0] = pair[0]
            resid_own[u, o, 1] = pair[1]
            resid_copy(u, o).start()
            fill(later_mat, 4 * unit * u + 2 * unit * o, 0, pair[0], pair[1])

    def gather_early(u):
        for o in range(2):
            resid_copy(u, o).wait_recv()
            fill(early_mat, 2 * unit * u, 2 * rows * o, resid_in[u, o, 0], resid_in[u, o, 1])

    def later_terms(u):
        def step(i, carry):
            at = pl.ds(pl.multiple_of(i * tile, tile), tile)
            other = near[E1:E2 + 1, :, rows_of(u), at].reshape(4 * unit, tile)
            term = lax.dot_general(later_mat[4 * unit * u:4 * unit * (u + 1), :], other,
                                   (((0,), (0,)), ((), ())),
                                   preferred_element_type=jnp.float32).reshape(2, rows, tile)
            share = jnp.sum(own[:, :, at].astype(jnp.float32) * term, axis=(0, 1)).reshape(1, tile)
            if u == 0:
                acc[:, :, at] = term
                parts[me, :, at] = share
            else:
                acc[:, :, at] += term
                parts[me, :, at] += share
            return carry

        lax.fori_loop(0, cols // tile, step, 0)

    def early_terms(first, last):
        def step(i, carry):
            at = pl.ds(pl.multiple_of(i * tile, tile), tile)
            other = near[L1:L2 + 1, :, :, at].reshape(4 * rows, tile)
            term = jnp.dot(early_mat[2 * unit * first:2 * unit * last, :], other,
                           preferred_element_type=jnp.float32)
            for u in range(first, last):
                for part in range(2):
                    low = (2 * (u - first) + part) * unit
                    acc[part, rows_of(u), at] += term[low:low + unit]
            return carry

        lax.fori_loop(0, cols // tile, step, 0)

    for t in range(CHUNKS):
        to_mate(t).start()
    for h in range(HALVES):
        to_sib(h).start()
    for copy in loads:
        copy.wait()
    weighted[...] = (own[...].astype(jnp.float32) * weight[...].reshape(1, 1, cols)).astype(
        jnp.bfloat16).reshape(2 * rows, cols)
    for o in range(2):
        amp_t[o] = amp_in[o].T * used[0, o].astype(jnp.float32)
        for part in range(2):
            obs_t[o, part] = obs_in[o, part].T
    for h in range(HALVES):
        got_sib(h)

    per_unit = CHUNKS // UNITS

    def far_step(t):
        to_far(t).wait_recv()

        @pl.when(jnp.logical_not(pass_is_mate))
        def _():
            to_pass(t).start()

        if (t + 1) % per_unit == 0:
            u = t // per_unit
            for v in range(u * per_unit, (u + 1) * per_unit):
                got_pass(v)
            correlate(u)
            if u > 0:
                residual(u - 1)
                later_terms(u - 1)

    for t in range(CHUNKS):
        got_mate(t)
        to_far(t).start()

        @pl.when(pass_is_mate)
        def _():
            to_pass(t).start()

        if t >= LAG:
            far_step(t - LAG)
    for t in range(CHUNKS - LAG, CHUNKS):
        far_step(t)
    for u in range(UNITS - 1):
        gather_early(u)
    early_terms(0, UNITS - 1)
    residual(UNITS - 1)
    later_terms(UNITS - 1)

    def part_copy(step):
        target = lax.rem(me + step, n)
        return remote(parts.at[me], parts.at[me], part_send.at[step], part_recv.at[me], target, gx)

    def part_start(step, carry):
        part_copy(step).start()
        return carry

    lax.fori_loop(1, n, part_start, 0)
    gather_early(UNITS - 1)
    early_terms(UNITS - 1, UNITS)

    def part_wait(step, carry):
        source = lax.rem(me + step, n)
        remote(parts.at[me], parts.at[source], part_send.at[step], part_recv.at[source], source, gx).wait()
        return carry

    lax.fori_loop(1, n, part_wait, 0)

    def add_part(i, total):
        return total + parts[i]

    kernel_out[...] = kernel_scale * lax.fori_loop(1, n, add_part, parts[0])

    for t in range(CHUNKS):
        to_mate(t).wait_send()
        to_far(t).wait_send()
        to_pass(t).wait_send()
    for h in range(HALVES):
        to_sib(h).wait_send()
    for u in range(UNITS):
        for o in range(2):
            resid_copy(u, o).wait_send()


def shards(green, source_weight, observed, amp_weight, pair_used):
    rows, cols = green.shape[1], green.shape[2]
    n = lax.axis_size("cable")
    ng = lax.axis_size("grid")
    inv_norm = 1.0 / math.sqrt(cols * ng)
    kernel_scale = inv_norm / (2.0 * math.sqrt(2.0 * n))
    unit = rows // UNITS
    peers = max(ng - 1, 1)
    f32, bf16 = jnp.float32, jnp.bfloat16
    dma = pltpu.SemaphoreType.DMA
    vmem = pl.BlockSpec(memory_space=pltpu.VMEM)
    hbm = pl.BlockSpec(memory_space=pl.ANY)
    fields, kernel = pl.pallas_call(
        functools.partial(body, (n, ng, inv_norm, kernel_scale)),
        out_shape=(pltpu.VMEM((2, rows, cols), f32), jax.ShapeDtypeStruct((1, cols), f32)),
        in_specs=[hbm, vmem, hbm, hbm, pl.BlockSpec(memory_space=pltpu.SMEM)],
        out_specs=(vmem, vmem),
        scratch_shapes=[
            pltpu.VMEM((2, rows, cols), bf16),
            pltpu.VMEM((2, 2, rows, rows), f32),
            pltpu.VMEM((2, rows, rows), f32),
            pltpu.VMEM((2, 2, rows, rows), f32),
            pltpu.VMEM((2, rows, rows), f32),
            pltpu.VMEM((4, 2, rows, cols), bf16),
            pltpu.VMEM((2 * rows, cols), bf16),
            pltpu.VMEM((UNITS, 2, 2, unit, rows), f32),
            pltpu.VMEM((UNITS, peers, 2, 2, unit, rows), f32),
            pltpu.VMEM((UNITS, 2, 2, unit, rows), bf16),
            pltpu.VMEM((UNITS, 2, 2, unit, rows), bf16),
            pltpu.VMEM((4 * rows, 2 * rows), bf16),
            pltpu.VMEM((2 * rows, 4 * rows), bf16),
            pltpu.VMEM((n, 1, cols), f32),
            dma((CHUNKS,)), dma((CHUNKS,)),
            dma((HALVES,)), dma((HALVES,)),
            dma((CHUNKS,)), dma((CHUNKS,)),
            dma((CHUNKS,)), dma((CHUNKS,)),
            dma((UNITS, peers)), dma((UNITS, peers)),
            dma((UNITS, 2)), dma((UNITS, 2)),
            dma((n,)), dma((n,)),
            dma((3,)),
        ],
        compiler_params=pltpu.CompilerParams(
            collective_id=0, has_side_effects=True, vmem_limit_bytes=56 * 1024 * 1024),
        cost_estimate=pl.CostEstimate(flops=24 * rows * rows * cols * 2, bytes_accessed=20 * rows * cols, transcendentals=0),
    )(green, source_weight.reshape(1, cols), observed, amp_weight, pair_used)
    adjoint = (inv_norm * fields) * source_weight[None, None, :]
    return (adjoint, kernel.reshape(cols))


def solution(mesh):
    in_specs = (
        P(None, "cable", "grid"),
        P("grid"),
        P(None, None, "cable", None),
        P(None, "cable", None),
        P("cable", None),
    )
    out_specs = (P(None, "cable", "grid"), P("grid"))
    return jax.shard_map(shards, mesh=mesh, in_specs=in_specs, out_specs=out_specs, check_vma=False)
```

time: 95.4 us -> 84.3 us (0.88)
  Pallas kernels: 89.3 us -> 79.4 us
  local copies, waits for them, and re-layouts: 5.31 us -> 0.6 us
  other arithmetic: 0 us -> 3.41 us
    pallas_call x1, Pallas kernels: 89.3 us -> 79.4 us  [shards(): pl.pallas_call(functools.partial(body, (n, ng, inv_norm, kernel_scale)),...]
    unnamed x4 -> x3, local copies, waits for them, and re-layouts: 5.31 us -> 0.6 us
    mul x0 -> x2, other arithmetic: none -> 3.41 us  [shards(): adjoint = inv_norm * fields * source_weight[None, None, :]]
where the time goes in v2:
time: 84.3 us; the launch traced here: 84 us
  Pallas kernels  79.4 us (94%)
  other arithmetic  3.41 us (4%)
    pallas_call x1, Pallas kernels, shards(): pl.pallas_call(functools.partial(body, (n, ng, inv_norm, kernel_scale)),...  79.4 us
    mul x2, other arithmetic, shards(): adjoint = inv_norm * fields * source_weight[None, None, :]  3.41 us

profile of v2, /device:TPU:0, one launch (start us, length us, event | category | flops | bytes accessed | tf_op | source)
XLA Modules:
  0.0 84.0 jit_solution(12820251153988599623)
XLA Ops:
  0.6 0.7 broadcast_multiply_fusion.1
  1.3 79.4 %shard_map.68 = (f32[2,256,2048]{2,1,0:T(8,128)S(1)}, f32[1,2048]{1,0:T(1,128)}) custom-call(bf16[2,256,2048]{2,1,0:T(8,128)(2,1)} %green.1, f32[1,2048]{1,0:T(1,128)} %bitcast.2, f32[2,2,256,256]{3,2,1,0:T(8,128)} %observed.1, f32[2,256,256]{2,1,0:T(8,128)} %amp.1, s32[1,2]{1,0:T(1,128)} %used.1), custom_call_target="tpu_custom_call" | custom-call | flops 6442450944 | bytes 10485760 | tf_op jit(solution)/shard_map/pallas_call | solution.py:279
  80.7 0.0 copy-start
  80.7 2.7 %broadcast_multiply_fusion = f32[2,256,2048]{2,1,0:T(8,128)} fusion(f32[2,256,2048]{2,1,0:T(8,128)S(1)} %get-tuple-element.4, f32[2048]{0:T(1024)S(1)} %broadcast_multiply_fusion.1), kind=kLoop, calls=%fused_computation | loop fusion | flops 1048576 | bytes 8396800 | tf_op jit(solution)/shard_map/mul | solution.py:312
  83.4 0.0 copy-done
  83.4 0.6 copy.8
Async XLA Ops:
  80.7 2.7 %copy-start = (f32[1,2048]{1,0:T(1,128)S(1)}, f32[1,2048]{1,0:T(1,128)}, u32[]{:S(2)}) copy-start(f32[1,2048]{1,0:T(1,128)} %get-tuple-element.5) | copy-start | bytes 24580

commit v3 on v2

--- a/solution.py
+++ b/solution.py
@@ -11,19 +11,21 @@
 MESH = pl.DeviceIdType.MESH
 E1, E2, L1, L2 = 0, 1, 2, 3
 CHUNKS = 16
-UNITS = 4
+SIZES = (7, 4, 3, 2)
+UNITS = len(SIZES)
 HALVES = 2
 LAG = 3
 
 
-def body(cfg, green, weight, observed, amp, used, acc, kernel_out,
+def body(cfg, green, weight, observed, amp, used, acc, kernel_out, scale_out,
          own, obs_in, amp_in, obs_t, amp_t, near, weighted, corr_own, corr_in, resid_own, resid_in, later_mat, early_mat, parts,
          mate_send, mate_recv, sib_send, sib_recv, far_send, far_recv, pass_send, pass_recv,
          corr_send, corr_recv, resid_send, resid_recv, part_send, part_recv, load_sem):
     n, ng, inv_norm, kernel_scale = cfg
     rows, cols = green.shape[1], green.shape[2]
     half_rows = rows // HALVES
-    unit = rows // UNITS
+    sizes = [size * rows // sum(SIZES) for size in SIZES]
+    begins = [sum(sizes[:u]) for u in range(UNITS)]
     chunk_rows = rows // CHUNKS
     tile = min(512, cols)
     me = lax.axis_index("cable")
@@ -57,7 +59,7 @@
     pl.semaphore_wait(barrier, n - 1 + ng - 1)
 
     def rows_of(u):
-        return slice(u * unit, (u + 1) * unit)
+        return slice(begins[u], begins[u] + sizes[u])
 
     def chunk(t):
         return pl.ds(t * chunk_rows, chunk_rows)
@@ -98,59 +100,65 @@
                pass_send.at[t], pass_recv.at[t], sibling, gx).wait_recv()
 
     def corr_copy(u, step):
-        return remote(corr_own.at[u], corr_in.at[u, step - 1],
+        return remote(corr_own.at[:, :, rows_of(u), :], corr_in.at[step - 1, :, :, rows_of(u), :],
                       corr_send.at[u, step - 1], corr_recv.at[u, step - 1],
                       me, lax.rem(gx + step, ng))
 
     def resid_copy(u, o):
-        return remote(resid_own.at[u, o], resid_in.at[u, o],
+        return remote(resid_own.at[o, :, rows_of(u), :], resid_in.at[o, :, rows_of(u), :],
                       resid_send.at[u, o], resid_recv.at[u, o],
                       lax.rem(me - (o + 1) + n, n), gx)
 
     def correlate(u):
+        unit = sizes[u]
         other = near[E1:E2 + 1, :, rows_of(u), :].reshape(4 * unit, cols)
         prod = lax.dot_general(other, weighted[...], (((1,), (1,)), ((), ())),
                                preferred_element_type=jnp.float32)
         for o in range(2):
             from_real = prod[2 * o * unit:(2 * o + 1) * unit]
             from_imag = prod[(2 * o + 1) * unit:(2 * o + 2) * unit]
-            corr_own[u, o, 0] = from_real[:, :rows] + from_imag[:, rows:]
-            corr_own[u, o, 1] = from_imag[:, :rows] - from_real[:, rows:]
+            corr_own[o, 0, rows_of(u), :] = from_real[:, :rows] + from_imag[:, rows:]
+            corr_own[o, 1, rows_of(u), :] = from_imag[:, :rows] - from_real[:, rows:]
         for step in range(1, ng):
             corr_copy(u, step).start()
 
-    def fill(mat, top, left, real, imag):
+    def fill(mat, unit, top, low, left, real, imag):
         mat[top:top + unit, left:left + rows] = real
         mat[top:top + unit, left + rows:left + 2 * rows] = -imag
-        mat[top + unit:top + 2 * unit, left:left + rows] = imag
-        mat[top + unit:top + 2 * unit, left + rows:left + 2 * rows] = real
+        mat[low:low + unit, left:left + rows] = imag
+        mat[low:low + unit, left + rows:left + 2 * rows] = real
 
     def residual(u):
+        unit = sizes[u]
         for step in range(1, ng):
             corr_copy(u, step).wait()
         for o in range(2):
             pair = []
             for part in range(2):
-                total = corr_own[u, o, part]
+                total = corr_own[o, part, rows_of(u), :]
                 for step in range(1, ng):
-                    total = total + corr_in[u, step - 1, o, part]
+                    total = total + corr_in[step - 1, o, part, rows_of(u), :]
                 value = amp_t[o, rows_of(u), :] * (inv_norm * total - obs_t[o, part, rows_of(u), :])
                 pair.append(value.astype(jnp.bfloat16))
-            resid_own[u, o, 0] = pair[0]
-            resid_own[u, o, 1] = pair[1]
+            resid_own[o, 0, rows_of(u), :] = pair[0]
+            resid_own[o, 1, rows_of(u), :] = pair[1]
             resid_copy(u, o).start()
-            fill(later_mat, 4 * unit * u + 2 * unit * o, 0, pair[0], pair[1])
+            top = 4 * begins[u] + 2 * unit * o
+            fill(later_mat, unit, top, top + unit, 0, pair[0], pair[1])
 
     def gather_early(u):
         for o in range(2):
             resid_copy(u, o).wait_recv()
-            fill(early_mat, 2 * unit * u, 2 * rows * o, resid_in[u, o, 0], resid_in[u, o, 1])
+            fill(early_mat, sizes[u], begins[u], rows + begins[u], 2 * rows * o,
+                 resid_in[o, 0, rows_of(u), :], resid_in[o, 1, rows_of(u), :])
 
     def later_terms(u):
+        unit = sizes[u]
+        top = 4 * begins[u]
         def step(i, carry):
             at = pl.ds(pl.multiple_of(i * tile, tile), tile)
             other = near[E1:E2 + 1, :, rows_of(u), at].reshape(4 * unit, tile)
-            term = lax.dot_general(later_mat[4 * unit * u:4 * unit * (u + 1), :], other,
+            term = lax.dot_general(later_mat[top:top + 4 * unit, :], other,
                                    (((0,), (0,)), ((), ())),
                                    preferred_element_type=jnp.float32).reshape(2, rows, tile)
             share = jnp.sum(own[:, :, at].astype(jnp.float32) * term, axis=(0, 1)).reshape(1, tile)
@@ -164,16 +172,12 @@
 
         lax.fori_loop(0, cols // tile, step, 0)
 
-    def early_terms(first, last):
+    def early_terms():
         def step(i, carry):
             at = pl.ds(pl.multiple_of(i * tile, tile), tile)
             other = near[L1:L2 + 1, :, :, at].reshape(4 * rows, tile)
-            term = jnp.dot(early_mat[2 * unit * first:2 * unit * last, :], other,
-                           preferred_element_type=jnp.float32)
-            for u in range(first, last):
-                for part in range(2):
-                    low = (2 * (u - first) + part) * unit
-                    acc[part, rows_of(u), at] += term[low:low + unit]
+            acc[:, :, at] += jnp.dot(early_mat[...], other,
+                                     preferred_element_type=jnp.float32).reshape(2, rows, tile)
             return carry
 
         lax.fori_loop(0, cols // tile, step, 0)
@@ -182,6 +186,7 @@
         to_mate(t).start()
     for h in range(HALVES):
         to_sib(h).start()
+    scale_out[...] = inv_norm * weight[...]
     for copy in loads:
         copy.wait()
     weighted[...] = (own[...].astype(jnp.float32) * weight[...].reshape(1, 1, cols)).astype(
@@ -193,8 +198,6 @@
     for h in range(HALVES):
         got_sib(h)
 
-    per_unit = CHUNKS // UNITS
-
     def far_step(t):
         to_far(t).wait_recv()
 
@@ -202,14 +205,14 @@
         def _():
             to_pass(t).start()
 
-        if (t + 1) % per_unit == 0:
-            u = t // per_unit
-            for v in range(u * per_unit, (u + 1) * per_unit):
-                got_pass(v)
-            correlate(u)
-            if u > 0:
-                residual(u - 1)
-                later_terms(u - 1)
+        for u in range(UNITS):
+            if (t + 1) * chunk_rows == begins[u] + sizes[u]:
+                for v in range(begins[u] // chunk_rows, t + 1):
+                    got_pass(v)
+                correlate(u)
+                if u > 0:
+                    residual(u - 1)
+                    later_terms(u - 1)
 
     for t in range(CHUNKS):
         got_mate(t)
@@ -225,7 +228,6 @@
         far_step(t)
     for u in range(UNITS - 1):
         gather_early(u)
-    early_terms(0, UNITS - 1)
     residual(UNITS - 1)
     later_terms(UNITS - 1)
 
@@ -239,7 +241,7 @@
 
     lax.fori_loop(1, n, part_start, 0)
     gather_early(UNITS - 1)
-    early_terms(UNITS - 1, UNITS)
+    early_terms()
 
     def part_wait(step, carry):
         source = lax.rem(me + step, n)
@@ -270,17 +272,16 @@
     ng = lax.axis_size("grid")
     inv_norm = 1.0 / math.sqrt(cols * ng)
     kernel_scale = inv_norm / (2.0 * math.sqrt(2.0 * n))
-    unit = rows // UNITS
     peers = max(ng - 1, 1)
     f32, bf16 = jnp.float32, jnp.bfloat16
     dma = pltpu.SemaphoreType.DMA
     vmem = pl.BlockSpec(memory_space=pltpu.VMEM)
     hbm = pl.BlockSpec(memory_space=pl.ANY)
-    fields, kernel = pl.pallas_call(
+    fields, kernel, scale = pl.pallas_call(
         functools.partial(body, (n, ng, inv_norm, kernel_scale)),
-        out_shape=(pltpu.VMEM((2, rows, cols), f32), jax.ShapeDtypeStruct((1, cols), f32)),
+        out_shape=(pltpu.VMEM((2, rows, cols), f32), jax.ShapeDtypeStruct((1, cols), f32), pltpu.VMEM((1, cols), f32)),
         in_specs=[hbm, vmem, hbm, hbm, pl.BlockSpec(memory_space=pltpu.SMEM)],
-        out_specs=(vmem, vmem),
+        out_specs=(vmem, vmem, vmem),
         scratch_shapes=[
             pltpu.VMEM((2, rows, cols), bf16),
             pltpu.VMEM((2, 2, rows, rows), f32),
@@ -289,10 +290,10 @@
             pltpu.VMEM((2, rows, rows), f32),
             pltpu.VMEM((4, 2, rows, cols), bf16),
             pltpu.VMEM((2 * rows, cols), bf16),
-            pltpu.VMEM((UNITS, 2, 2, unit, rows), f32),
-            pltpu.VMEM((UNITS, peers, 2, 2, unit, rows), f32),
-            pltpu.VMEM((UNITS, 2, 2, unit, rows), bf16),
-            pltpu.VMEM((UNITS, 2, 2, unit, rows), bf16),
+            pltpu.VMEM((2, 2, rows, rows), f32),
+            pltpu.VMEM((peers, 2, 2, rows, rows), f32),
+            pltpu.VMEM((2, 2, rows, rows), bf16),
+            pltpu.VMEM((2, 2, rows, rows), bf16),
             pltpu.VMEM((4 * rows, 2 * rows), bf16),
             pltpu.VMEM((2 * rows, 4 * rows), bf16),
             pltpu.VMEM((n, 1, cols), f32),
@@ -309,7 +310,7 @@
             collective_id=0, has_side_effects=True, vmem_limit_bytes=56 * 1024 * 1024),
         cost_estimate=pl.CostEstimate(flops=24 * rows * rows * cols * 2, bytes_accessed=20 * rows * cols, transcendentals=0),
     )(green, source_weight.reshape(1, cols), observed, amp_weight, pair_used)
-    adjoint = (inv_norm * fields) * source_weight[None, None, :]
+    adjoint = fields * scale[None, :, :]
     return (adjoint, kernel.reshape(cols))
 
 

time: 84.3 us -> 80.7 us (0.957)
  Pallas kernels: 79.4 us -> 76.5 us
    pallas_call x1, Pallas kernels: 79.4 us -> 76.5 us  [shards(): pl.pallas_call(functools.partial(body, (n, ng, inv_norm, kernel_scale)),...]
    mul x2 -> x1, other arithmetic: 3.41 us -> 2.7 us  [shards(): adjoint = fields * scale[None, :, :]]
where the time goes in v3:
time: 80.7 us; the launch traced here: 80.4 us
  Pallas kernels  76.5 us (95%)
  other arithmetic  2.7 us (3%)
    pallas_call x1, Pallas kernels, shards(): pl.pallas_call(functools.partial(body, (n, ng, inv_norm, kernel_scale)),...  76.5 us
    mul x1, other arithmetic, shards(): adjoint = fields * scale[None, :, :]  2.7 us

profile of v3, /device:TPU:0, one launch (start us, length us, event | category | flops | bytes accessed | tf_op | source)
XLA Modules:
  0.0 80.4 jit_solution(5216453754499202479)
XLA Ops:
  0.6 76.5 %shard_map.68 = (f32[2,256,2048]{2,1,0:T(8,128)S(1)}, f32[1,2048]{1,0:T(1,128)}, f32[1,2048]{1,0:T(1,128)S(1)}) custom-call(bf16[2,256,2048]{2,1,0:T(8,128)(2,1)} %green.1, f32[1,2048]{1,0:T(1,128)} %bitcast.5, f32[2,2,256,256]{3,2,1,0:T(8,128)} %observed.1, f32[2,256,256]{2,1,0:T(8,128)} %amp.1, s32[1,2]{1,0:T(1,128)} %used.1), custom_call_target="tpu_custom_call" | custom-call | flops 6442450944 | bytes 10485760 | tf_op jit(solution)/shard_map/pallas_call | solution.py:280
  77.1 0.0 copy-start
  77.1 2.7 %broadcast_multiply_fusion = f32[2,256,2048]{2,1,0:T(8,128)} fusion(f32[2,256,2048]{2,1,0:T(8,128)S(1)} %get-tuple-element.5, f32[2048]{0:T(1024)S(1)} %bitcast.3), kind=kLoop, calls=%fused_computation | loop fusion | flops 1048576 | bytes 8396800 | tf_op jit(solution)/shard_map/mul | solution.py:313
  79.8 0.0 copy-done
  79.8 0.6 copy.8
Async XLA Ops:
  77.1 2.7 %copy-start = (f32[1,2048]{1,0:T(1,128)S(1)}, f32[1,2048]{1,0:T(1,128)}, u32[]{:S(2)}) copy-start(f32[1,2048]{1,0:T(1,128)} %get-tuple-element.7) | copy-start | bytes 24580
